TPU v7x, 512 devices: a whole 4x8x8 slice. The times are simulated.
512 devices in a mesh: row: 32 (over z, x), col: 16 (over y, core).
Axes of the slice: x: 4, y: 8, z: 8, core: 2. Of those that a mesh axis runs over, the one named last changes fastest.
Arguments:
- hidden: bfloat16 [4096, 12288], P('row', 'col'), may hold values from -6 to 6
- w_down: bfloat16 [12288, 4096], P('row', 'col'), may hold values from -0.0546875 to 0.0546875
- stream_in: bfloat16 [4096, 4096], P('row', 'col'), may hold values from -6 to 6
- w_qkv: bfloat16 [4096, 12288], P('row', 'col'), may hold values from -0.09375 to 0.09375
Outputs:
- stream: bfloat16 [4096, 4096], P('row', 'col')
- attended: bfloat16 [4096, 4096], P('row', 'col')
All inputs are finite; a program needn't handle non-finite values.
Results may differ from a plain program's by a relative error of at most 0.015.
Values may be sent and summed in bfloat16 or wider, within the bound.
A program may use at most 64 MiB of HBM per device.

v0:
```python
import jax
import jax.numpy as jnp
from jax import lax
from jax.sharding import PartitionSpec as P

D_W = 4096
HEAD = 128


EPSILON = 1e-06


def partner(shard, axis, apart):
    return lax.ppermute(shard, axis, [(i, i ^ 1 << apart) for i in range(lax.axis_size(axis))])


def head_norm(parts):
    centre = parts - jnp.mean(parts, axis=-1, keepdims=True)
    spread = jnp.mean(centre * centre, axis=-1, keepdims=True)
    return centre * lax.rsqrt(spread + EPSILON)


def normalize(stream_f32, row_mean, row_var):
    return ((stream_f32 - row_mean[:, None]) * lax.rsqrt(row_var + EPSILON)[:, None]).astype(
        jnp.bfloat16
    )


def shards(hidden, w_down, stream_in, w_qkv):
    tok_rows = hidden.shape[0]
    whole_hidden = lax.all_gather(hidden, "col", axis=1, tiled=True)
    columns = whole_hidden
    mlp_out = jnp.dot(
        columns,
        lax.all_gather(w_down, "row", axis=0, tiled=True),
        preferred_element_type=jnp.float32,
    )
    stream = (stream_in.astype(jnp.float32) + mlp_out).astype(jnp.bfloat16)
    stream_f32 = stream.astype(jnp.float32)
    row_total, row_square = lax.psum(
        (jnp.sum(stream_f32, axis=1), jnp.sum(stream_f32 * stream_f32, axis=1)), "col"
    )
    row_mean = row_total / D_W
    row_var = row_square / D_W - row_mean * row_mean
    normed = lax.all_gather(normalize(stream_f32, row_mean, row_var), "col", axis=1, tiled=True)
    columns = normed
    qkv = jnp.dot(
        columns,
        lax.all_gather(w_qkv, "row", axis=0, tiled=True),
        preferred_element_type=jnp.float32,
    )
    head_count = w_qkv.shape[1] // (3 * HEAD)
    qkv = qkv.reshape(tok_rows, head_count, 3, HEAD)
    queries = (head_norm(qkv[:, :, 0]) * (1.0 / HEAD**0.5)).astype(jnp.bfloat16)
    keys_local = head_norm(qkv[:, :, 1]).astype(jnp.bfloat16)
    values_local = qkv[:, :, 2].astype(jnp.bfloat16)
    keys_other, values_other = partner((keys_local, values_local), "row", 0)
    all_keys = jnp.concatenate([keys_local, keys_other], axis=0)
    all_values = jnp.concatenate([values_local, values_other], axis=0)
    scores = jnp.einsum("qhe,khe->hqk", queries, all_keys, preferred_element_type=jnp.float32)
    expon = jnp.exp(scores)
    probs = (expon / jnp.sum(expon, axis=-1, keepdims=True)).astype(jnp.bfloat16)
    attended = jnp.einsum("hqk,khe->qhe", probs, all_values, preferred_element_type=jnp.float32)
    return (stream, attended.reshape(tok_rows, head_count * HEAD).astype(jnp.bfloat16))


def solution(mesh):
    placed = (P("row", "col"), P("row", "col"), P("row", "col"), P("row", "col"))
    return jax.shard_map(
        shards,
        mesh=mesh,
        in_specs=placed,
        out_specs=(P("row", "col"), P("row", "col")),
        check_vma=False,
    )
```

profile of v0, /device:TPU:1, one launch (start us, length us, event | category | flops | bytes accessed | tf_op | source)
XLA Modules:
  0.0 312.2 jit_solution(5972452985936823533)
XLA Ops:
  7.2 0.0 all-gather.5.cloned.1.call-start
  7.2 0.7 all-gather.5.cloned.1.call-update
  7.9 0.0 all-gather.7.cloned.1.call-start
  7.9 0.7 all-gather.7.cloned.1.call-update
  8.6 0.0 all-gather.11.cloned.1.call-start
  8.7 0.7 all-gather.11.cloned.1.call-update
  9.4 0.0 all-gather.9.cloned.1.call-start
  9.4 50.2 %all-gather.5.cloned.1.call-done = bf16[128,12288]{1,0:T(8,128)(2,1)} async-done(((bf16[128,768]{1,0:T(8,128)(2,1)}), bf16[128,12288]{1,0:T(8,128)(2,1)}) %all-gather.5.cloned.1.call-update) | async-done | bytes 3145744 | tf_op jit(solution)/shard_map/all_gather | solution.py:31
  59.6 96.1 %all-gather.7.cloned.1.call-done = bf16[12288,256]{1,0:T(8,128)(2,1)} async-done(((bf16[384,256]{1,0:T(8,128)(2,1)}), bf16[12288,256]{1,0:T(8,128)(2,1)}) %all-gather.7.cloned.1.call-update) | async-done | bytes 6291472 | tf_op jit(solution)/shard_map/all_gather | solution.py:35
  155.7 4.8 %convert_reduce_fusion = (f32[128]{0:T(128)S(1)}, f32[128]{0:T(128)S(1)}, bf16[128,256]{1,0:T(8,128)(2,1)S(1)}) fusion(bf16[128,12288]{1,0:T(8,128)(2,1)} %all-gather.5.cloned.1.call-done, bf16[12288,256]{1,0:T(8,128)(2,1)} %all-gather.7.cloned.1.call-done, bf16[128,256]{1,0:T(8,128)(2,1)} %param.6), kind=kOutput, calls=%fused_computation.7 | convolution fusion | flops 805535488 | bytes 9569280 | tf_op jit(solution)/shard_map/dot_general | solution.py:33
  160.5 0.0 copy-start
  160.5 23.9 %all-reduce = (f32[128]{0:T(128)S(1)}, f32[128]{0:T(128)S(1)}) all-reduce(f32[128]{0:T(128)S(1)} %get-tuple-element.9, f32[128]{0:T(128)S(1)} %get-tuple-element.8), channel_id=1, replica_groups=mesh['row'=32,'col'=16] {'col'}, use_global_device_ids=true, to_apply=%region_3.0 | all-reduce | flops 256 | bytes 2048 | tf_op jit(solution)/shard_map/psum | solution.py:40
  184.4 0.7 fusion.2
  185.1 0.0 all-gather.9.cloned.1.call-update
  185.1 65.1 %all-gather.11.cloned.1.call-done = bf16[4096,768]{1,0:T(8,128)(2,1)} async-done(((bf16[128,768]{1,0:T(8,128)(2,1)}), bf16[4096,768]{1,0:T(8,128)(2,1)}) %all-gather.11.cloned.1.call-update) | async-done | bytes 6291472 | tf_op jit(solution)/shard_map/all_gather | solution.py:49
  250.2 39.9 %all-gather.9.cloned.1.call-done = bf16[128,4096]{1,0:T(8,128)(2,1)} async-done(((bf16[128,256]{1,0:T(8,128)(2,1)}), bf16[128,4096]{1,0:T(8,128)(2,1)}) %all-gather.9.cloned.1.call-update) | async-done | bytes 1048592 | tf_op jit(solution)/shard_map/all_gather | solution.py:45
  290.1 5.7 %fusion.27 = f32[128,768]{0,1:T(8,128)S(1)} fusion(bf16[128,4096]{1,0:T(8,128)(2,1)} %all-gather.9.cloned.1.call-done, bf16[4096,768]{1,0:T(8,128)(2,1)} %all-gather.11.cloned.1.call-done), kind=kOutput, calls=%fused_computation.44 | convolution fusion | flops 805306368 | bytes 7733248 | tf_op jit(solution)/shard_map/dot_general | solution.py:47
  295.8 3.1 collective-permute-start
  298.9 0.1 copy.17
  299.0 0.2 multiply_reduce_fusion
  299.2 0.1 multiply_convert_fusion
  299.4 2.2 collective-permute-start.1
  301.6 2.8 collective-permute-done.1
  304.4 0.2 convolution_exponential_fusion
  304.6 0.0 collective-permute-done
  304.7 0.3 convolution_convert_fusion
  304.9 0.7 copy.14
  305.7 0.0 copy-done
  (8 shorter events, 0.1 us)
Async XLA Ops:
  7.2 52.4 %all-gather.5.cloned.1.call-start = ((), (), s32[]{:S(2)}) async-start(), calls=%async_computation | async-start | bytes 3342336 | tf_op jit(solution)/shard_map/all_gather | solution.py:31
  7.9 147.8 %all-gather.7.cloned.1.call-start = ((), (), s32[]{:S(2)}) async-start(), calls=%async_computation.1 | async-start | bytes 6488064 | tf_op jit(solution)/shard_map/all_gather | solution.py:35
  8.6 241.6 %all-gather.11.cloned.1.call-start = ((), (), s32[]{:S(2)}) async-start(), calls=%async_computation.3 | async-start | bytes 6488064 | tf_op jit(solution)/shard_map/all_gather | solution.py:49
  9.4 280.7 %all-gather.9.cloned.1.call-start = ((), (), s32[]{:S(2)}) async-start(), calls=%async_computation.2 | async-start | bytes 1114112 | tf_op jit(solution)/shard_map/all_gather | solution.py:45
  160.5 145.2 %copy-start = (bf16[128,256]{1,0:T(8,128)(2,1)}, bf16[128,256]{1,0:T(8,128)(2,1)S(1)}, u32[]{:S(2)}) copy-start(bf16[128,256]{1,0:T(8,128)(2,1)S(1)} %get-tuple-element.15) | copy-start | bytes 196612
  295.8 8.9 %collective-permute-start = (bf16[128,2,128]{0,2,1:T(8,128)(2,1)S(1)}, bf16[128,2,128]{0,2,1:T(8,128)(2,1)S(1)}, u32[]{:S(2)}, u32[]{:S(2)}) collective-permute-start(bf16[128,2,128]{0,2,1:T(8,128)(2,1)S(1)} %fusion.12), channel_id=1, source_target_pairs={{0,16},{16,0},{32,48},{48,32},{64,80},{80,64},{96,112},{112,96},{1... | collective-permute-start | bytes 196616 | tf_op jit(solution)/shard_map/ppermute | solution.py:14
  299.4 5.0 %collective-permute-start.1 = (bf16[128,2,128]{2,0,1:T(8,128)(2,1)S(1)}, bf16[128,2,128]{2,0,1:T(8,128)(2,1)S(1)}, u32[]{:S(2)}, u32[]{:S(2)}) collective-permute-start(bf16[128,2,128]{2,0,1:T(8,128)(2,1)S(1)} %multiply_convert_fusion), channel_id=1, source_target_pairs={{0,16},{16,0},{32,48},{48,32},{64,80},{80,64},{96,112},{112,96},{1... | collective-permute-start | bytes 196616 | tf_op jit(solution)/shard_map/ppermute | solution.py:14
Sparse Core Ops, SparseCore 0:
  10.1 49.4 all-gather.4
  62.8 92.9 all-gather.6
  158.9 91.2 all-gather.10
  252.7 37.3 all-gather.8
where the time goes:
time: 312 us
  waiting for transfers between devices  256 us (82%)
  blocking collectives  23.9 us (8%)
  between operations  13.9 us (4%)
  matrix products  11 us (4%)
  starting transfers between devices  5.43 us (2%)
    all_gather x1, waiting for transfers between devices, shards(): lax.all_gather(w_down, 'row', axis=0, tiled=True)  96.1 us
    all_gather x1, waiting for transfers between devices, shards(): lax.all_gather(w_qkv, 'row', axis=0, tiled=True)  65.1 us
    all_gather x1, waiting for transfers between devices, shards(): whole_hidden = lax.all_gather(hidden, 'col', axis=1, tiled=True)  50.2 us
    all_gather x1, waiting for transfers between devices, shards(): lax.all_gather(normalize(stream_f32, row_mean, row_var), 'col', axis=1, t...  39.9 us
    psum x1, blocking collectives, shards(): lax.psum((jnp.sum(stream_f32, axis=1), jnp.sum(stream_f32 * stream_f32, a...  23.9 us
  transfers between devices with their start and end apart: 6, of which 5 were waited for; matrix products, arithmetic and copies ran while one was open for 2% of the time, Pallas kernels for 0%

commit v1 on v0

v1 whole, which is shorter than its diff:
```python
import functools

import jax
import jax.numpy as jnp
from jax import lax
from jax.experimental import pallas as pl
from jax.experimental.pallas import tpu as pltpu
from jax.sharding import PartitionSpec as P

MESH = pl.DeviceIdType.MESH
EPSILON = 1e-06
D_W = 4096
HEAD = 128
NX, NY, NZ = 4, 8, 8
F32 = jnp.float32
BF16 = jnp.bfloat16


def head_norm(parts):
    centre = parts - jnp.mean(parts, axis=-1, keepdims=True)
    spread = jnp.mean(centre * centre, axis=-1, keepdims=True)
    return centre * lax.rsqrt(spread + EPSILON)


def kernel(
    hid, wd, si, wq, so, at,
    wdg, ag, p1, r1, sin, sg, st, stx, sty, wqg, p2, r2, ab,
    s_hid, r_hid, s_si, r_si, s_a, r_a, s_ac, r_ac, s_wd, r_wd, s_wq, r_wq, l_wd, l_wq,
    s_r1, r_r1, s_so, r_so, s_s, r_s, s_sc, r_sc, s_stx, r_stx, s_sty, r_sty, s_r2, r_r2, s_o, r_o,
):
    row, col = lax.axis_index("row"), lax.axis_index("col")
    z, x = lax.div(row, NX), lax.rem(row, NX)
    y, c = lax.div(col, 2), lax.rem(col, 2)
    xh, xl = lax.div(x, 2), lax.rem(x, 2)

    def dev(zz, xx, yy, cc):
        return (zz * NX + xx, yy * 2 + cc)

    up = lambda v, d, n: lax.rem(v + d + n, n)
    sibling = dev(z, x, y, 1 - c)
    yn = (dev(z, x, up(y, 1, NY), c), dev(z, x, up(y, -1, NY), c))
    zn = (dev(up(z, 1, NZ), x, y, c), dev(up(z, -1, NZ), x, y, c))
    xgroup = [dev(z, up(x, d, NX), y, e) for d in range(NX) for e in (c, 1 - c)][1:]
    ygroup = [dev(z, x, up(y, d, NY), c) for d in range(1, NY)]

    ends = []

    def remote(src, dst, ssem, rsem, to):
        copy = pltpu.make_async_remote_copy(
            src_ref=src, dst_ref=dst, send_sem=ssem, recv_sem=rsem, device_id=to, device_id_type=MESH
        )
        copy.start()
        ends.append((None, copy))

    def within(src, dst, ssem, rsem, tx, tc):
        away = (tx != x) | (tc != c)
        copy = pltpu.make_async_remote_copy(
            src_ref=src, dst_ref=dst, send_sem=ssem, recv_sem=rsem,
            device_id=dev(z, tx, y, tc), device_id_type=MESH,
        )

        @pl.when(away)
        def _():
            copy.start()

        @pl.when(jnp.logical_not(away))
        def _():
            pltpu.make_async_copy(src, dst, rsem).start()

        ends.append((away, copy))

    def arrived(dst, rsem):
        pltpu.make_async_remote_copy(
            src_ref=dst, dst_ref=dst, send_sem=rsem, recv_sem=rsem, device_id=sibling, device_id_type=MESH
        ).wait_recv()

    tok = lambda xt: pl.ds(pl.multiple_of(xt * 128, 128), 128)

    barrier = pltpu.get_barrier_semaphore()
    greet = xgroup + ygroup + list(zn)
    for d in greet:
        pl.semaphore_signal(barrier, inc=1, device_id=d, device_id_type=MESH)
    own_wd = pltpu.make_async_copy(wd, wdg.at[pl.ds(pl.multiple_of(z * 384, 128), 384)], l_wd.at[0])
    own_wd.start()
    own_wq = [
        pltpu.make_async_copy(
            wq.at[:, pl.ds(h * 384, 384)], wqg.at[h, pl.ds(pl.multiple_of(z * 128, 128), 128)], l_wq.at[h]
        )
        for h in range(2)
    ]
    for copy in own_wq:
        copy.start()
    pl.semaphore_wait(barrier, len(greet))

    def wd_piece(j, p):
        return wdg.at[pl.ds(pl.multiple_of(j * 384 + p * 192, 64), 192)]

    def wq_piece(j, p):
        return wqg.at[p, pl.ds(pl.multiple_of(j * 128, 128), 128)]

    def a_piece(j, i):
        return ag.at[j, tok(2 * i + c)]

    def s_piece(j, i):
        return sg.at[j, tok(2 * i + c)]

    def hop_send(piece, me, n, ssem, rsem, to, s, d, p, first=None):
        sign = 1 if d == 0 else -1
        j = up(me, -sign * (s - 1), n)
        k = (s - 1) * 4 + d * 2 + p
        remote(first(p) if s == 1 and first else piece(j, p), piece(j, p), ssem.at[k], rsem.at[k], to[d])

    def hop_wait(piece, me, n, rsem, s, d, p):
        sign = 1 if d == 0 else -1
        j = up(me, -sign * s, n)
        arrived(piece(j, p), rsem.at[(s - 1) * 4 + d * 2 + p])
        return j

    hops = lambda s: [(d, p) for p in range(2) for d in range(2) if s < 4 or d == p]

    for d, p in hops(1):
        hop_send(wd_piece, z, NZ, s_wd, r_wd, zn, 1, d, p, first=lambda p: wd.at[pl.ds(p * 192, 192)])
    for h in range(2):
        within(hid.at[:, pl.ds(h * 384, 384)], ag.at[y, tok(x)], s_hid.at[h], r_hid.at[xh], 2 * c + h, xl)
    for h in range(2):
        within(si.at[:, pl.ds(h * 128, 128)], sin.at[xh], s_si.at[h], r_si.at[xh], 2 * c + h, xl)
    for i in range(2):
        arrived(a_piece(y, i), r_hid.at[i])
        for d in range(2):
            hop_send(a_piece, y, NY, s_a, r_a, yn, 1, d, i)
        remote(a_piece(y, i), a_piece(y, i), s_ac.at[i], r_ac.at[i], sibling)

    def a_hop(s):
        for d, p in hops(s):
            j = hop_wait(a_piece, y, NY, r_a, s, d, p)
            if s < 4 and (s + 1 < 4 or d == p):
                hop_send(a_piece, y, NY, s_a, r_a, yn, s + 1, d, p)
            k = 2 + (s - 1) * 4 + d * 2 + p
            remote(a_piece(j, p), a_piece(j, p), s_ac.at[k], r_ac.at[k], sibling)

    def z_hop(piece, ssem, rsem, s):
        for d, p in hops(s):
            hop_wait(piece, z, NZ, rsem, s, d, p)
            if s < 4 and (s + 1 < 4 or d == p):
                hop_send(piece, z, NZ, ssem, rsem, zn, s + 1, d, p)

    for s in range(1, 5):
        z_hop(wd_piece, s_wd, r_wd, s)
        if s == 3:
            for copy in own_wq:
                copy.wait()
            for d, p in hops(1):
                hop_send(wq_piece, z, NZ, s_wq, r_wq, zn, 1, d, p)
        a_hop(s)
    own_wd.wait()

    def other_piece(j, i):
        return ag.at[j, tok(2 * i + 1 - c)]

    for i in range(2):
        arrived(other_piece(y, i), r_ac.at[i])
    for s in range(1, 5):
        for d, p in hops(s):
            j = up(y, -s if d == 0 else s, NY)
            arrived(other_piece(j, p), r_ac.at[2 + (s - 1) * 4 + d * 2 + p])

    for i in range(2):
        a = jnp.concatenate([ag[j, pl.ds(256 * i, 256), :] for j in range(NY)], axis=1)
        p1[pl.ds(256 * i, 256), :] = jnp.dot(a, wdg[...], preferred_element_type=F32).astype(BF16)
        for h in range(2):
            for e in range(2):
                within(
                    p1.at[tok(2 * i + e), pl.ds(128 * h, 128)], r1.at[x, i],
                    s_r1.at[i * 4 + h * 2 + e], r_r1.at[x * 2 + i], 2 * c + h, e,
                )

    z_hop(wq_piece, s_wq, r_wq, 1)

    lanes = lax.broadcasted_iota(jnp.int32, (8, 128), 0)
    ones = jnp.ones((8, 128), BF16)
    by_rows = lambda v: lax.dot_general(ones, v, (((1,), (1,)), ((), ())), preferred_element_type=F32)
    tile = jnp.zeros((8, 128), F32)
    for i in range(2):
        arrived(sin.at[i], r_si.at[i])
        total = sin[i].astype(F32)
        for xs in range(NX):
            arrived(r1.at[xs, i], r_r1.at[xs * 2 + i])
            total += r1[xs, i].astype(F32)
        block = total.astype(BF16)
        sg[y, tok(2 * i + c), :] = block
        for d in range(2):
            hop_send(s_piece, y, NY, s_s, r_s, yn, 1, d, i)
        remote(s_piece(y, i), s_piece(y, i), s_sc.at[i], r_sc.at[i], sibling)
        wide = block.astype(F32)
        square = wide * wide
        high = square.astype(BF16)
        low = (square - high.astype(F32)).astype(BF16)
        sums, squares = by_rows(block), by_rows(high) + by_rows(low)
        tile = jnp.where(lanes == i, sums, jnp.where(lanes == 2 + i, squares, tile))
    stx[c * 4 + x] = tile
    for n, d in enumerate(xgroup):
        remote(stx.at[c * 4 + x], stx.at[c * 4 + x], s_stx.at[n], r_stx.at[c * 4 + x], d)
    for i in range(2):
        within(s_piece(y, i), so.at[:, pl.ds(pl.multiple_of(128 * xl, 128), 128)], s_so.at[i], r_so.at[xl], 2 * i + c, xh)

    def s_hop(s):
        for d, p in hops(s):
            j = hop_wait(s_piece, y, NY, r_s, s, d, p)
            if s < 4 and (s + 1 < 4 or d == p):
                hop_send(s_piece, y, NY, s_s, r_s, yn, s + 1, d, p)
            k = 2 + (s - 1) * 4 + d * 2 + p
            remote(s_piece(j, p), s_piece(j, p), s_sc.at[k], r_sc.at[k], sibling)

    s_hop(1)
    for n in range(1, 2 * NX):
        k = lax.rem(c * 4 + x + n, 8)
        arrived(stx.at[k], r_stx.at[k])
    half = lambda k: (stx[4 * k] + stx[4 * k + 1]) + (stx[4 * k + 2] + stx[4 * k + 3])
    sty[y] = jnp.where(lanes < 4, half(0), jnp.concatenate([half(1)[4:8], half(1)[0:4]], axis=0))
    for n, d in enumerate(ygroup):
        remote(sty.at[y], sty.at[y], s_sty.at[n], r_sty.at[y], d)
    z_hop(wq_piece, s_wq, r_wq, 2)
    s_hop(2)
    s_hop(3)
    z_hop(wq_piece, s_wq, r_wq, 3)
    s_hop(4)
    for n in range(1, NY):
        k = lax.rem(y + n, NY)
        arrived(sty.at[k], r_sty.at[k])
    stats = sty[0]
    for j in range(1, NY):
        stats += sty[j]
    rows = []
    for xt in range(NX):
        i, k = xt // 2, xt % 2
        mean = stats[4 * k + i : 4 * k + i + 1] / D_W
        var = stats[4 * k + 2 + i : 4 * k + 3 + i] / D_W - mean * mean
        rows += [mean, lax.rsqrt(var + EPSILON)]
    st[...] = jnp.concatenate(rows + [jnp.zeros((120, 128), F32)], axis=0).T

    def other_s(j, i):
        return sg.at[j, tok(2 * i + 1 - c)]

    for i in range(2):
        arrived(other_s(y, i), r_sc.at[i])
    for s in range(1, 5):
        for d, p in hops(s):
            j = up(y, -s if d == 0 else s, NY)
            arrived(other_s(j, p), r_sc.at[2 + (s - 1) * 4 + d * 2 + p])
    z_hop(wq_piece, s_wq, r_wq, 4)

    for i in range(2):
        halves = []
        for k in range(2):
            xt = 2 * i + k
            mean, rstd = st[:, 2 * xt : 2 * xt + 1], st[:, 2 * xt + 1 : 2 * xt + 2]
            halves.append(
                jnp.concatenate(
                    [((sg[j, tok(xt), :].astype(F32) - mean) * rstd).astype(BF16) for j in range(NY)], axis=1
                )
            )
        normed = jnp.concatenate(halves, axis=0)
        for h in range(2):
            p2[h, i] = jnp.dot(normed, wqg[h], preferred_element_type=F32).astype(BF16)
            within(p2.at[h, i], r2.at[x], s_r2.at[2 * i + h], r_r2.at[x], 2 * c + h, i)

    total = jnp.zeros((256, 384), F32)
    for xs in range(NX):
        arrived(r2.at[xs], r_r2.at[xs])
        total += r2[xs].astype(F32)
    queries = (head_norm(total[:, 0:128]) * (1.0 / HEAD**0.5)).astype(BF16)
    keys = head_norm(total[:, 128:256]).astype(BF16)
    values = total[:, 256:384].astype(BF16)
    scores = lax.dot_general(queries, keys, (((1,), (1,)), ((), ())), preferred_element_type=F32)
    expon = jnp.exp(scores)
    probs = (expon / jnp.sum(expon, axis=-1, keepdims=True)).astype(BF16)
    ab[...] = jnp.dot(probs, values, preferred_element_type=F32).astype(BF16)
    for t in range(2):
        within(
            ab.at[pl.ds(128 * t, 128)], at.at[:, pl.ds(pl.multiple_of(128 * xl, 128), 128)],
            s_o.at[t], r_o.at[xl], 2 * c + t, xh,
        )

    for h in range(2):
        arrived(so.at[:, pl.ds(128 * h, 128)], r_so.at[h])
        arrived(at.at[:, pl.ds(128 * h, 128)], r_o.at[h])
    for away, copy in ends:
        if away is None:
            copy.wait_send()
        else:

            @pl.when(away)
            def _(copy=copy):
                copy.wait_send()


def shards(hidden, w_down, stream_in, w_qkv):
    dma = lambda *n: pltpu.SemaphoreType.DMA(n)
    vm = lambda *n: pltpu.VMEM(n, BF16)
    fm = lambda *n: pltpu.VMEM(n, F32)
    return pl.pallas_call(
        kernel,
        out_shape=(jax.ShapeDtypeStruct((128, 256), BF16), jax.ShapeDtypeStruct((128, 256), BF16)),
        in_specs=[pl.BlockSpec(memory_space=pltpu.VMEM)] * 4,
        out_specs=(pl.BlockSpec(memory_space=pltpu.VMEM),) * 2,
        scratch_shapes=[
            vm(3072, 256), vm(NY, 512, 384), vm(512, 256), vm(NX, 2, 128, 128), vm(2, 128, 128), vm(NY, 512, 128),
            fm(128, 128), fm(8, 8, 128), fm(NY, 8, 128), vm(2, 1024, 384), vm(2, 2, 256, 384), vm(NX, 256, 384),
            vm(256, 128),
            dma(2), dma(2), dma(2), dma(2), dma(16), dma(16), dma(18), dma(18), dma(16), dma(16), dma(16), dma(16),
            dma(1), dma(2),
            dma(8), dma(8), dma(2), dma(2), dma(16), dma(16), dma(18), dma(18), dma(7), dma(8), dma(7), dma(8),
            dma(4), dma(4), dma(2), dma(2),
        ],
        compiler_params=pltpu.CompilerParams(
            collective_id=0, has_side_effects=True, vmem_limit_bytes=40 * 1024 * 1024
        ),
        cost_estimate=pl.CostEstimate(flops=1_700_000_000, bytes_accessed=1_000_000, transcendentals=65536),
        name="layer",
    )(hidden, w_down, stream_in, w_qkv)


def solution(mesh):
    placed = (P("row", "col"),) * 4
    return jax.shard_map(
        shards, mesh=mesh, in_specs=placed, out_specs=(P("row", "col"), P("row", "col")), check_vma=False
    )
```

time: 312 us -> 82.2 us (0.26)
  waiting for transfers between devices: 256 us -> 0 us
  Pallas kernels: 0 us -> 76.1 us
  blocking collectives: 23.9 us -> 0 us
  between operations: 13.9 us -> 0.65 us
  matrix products: 11 us -> 0 us
  starting transfers between devices: 5.43 us -> 0 us
  local copies, waits for them, and re-layouts: 0.86 us -> 4.87 us
    all_gather x4 -> x0, waiting for transfers between devices: 251 us -> none  [the longest x1 96.1 us: shards(): lax.all_gather(w_down, 'row', axis=0, tiled=True)]
    pallas_call x0 -> x1, Pallas kernels: none -> 76.1 us  [shards(): pl.pallas_call(kernel, out_shape=(jax.ShapeDtypeStruct((128, 256), BF16),...]
    psum x1 -> x0, blocking collectives: 23.9 us -> none  [shards(): lax.psum((jnp.sum(stream_f32, axis=1), jnp.sum(stream_f32 * stream_f32, a...]
    dot_general x4 -> x0, matrix products: 11 us -> none  [the longest x1 5.66 us: shards(): jnp.dot(columns, lax.all_gather(w_qkv, 'row', axis=0, tiled=True), prefer...]
    ppermute x2 -> x0, starting transfers between devices: 5.28 us -> none  [partner(): lax.ppermute(shard, axis, [(i, i ^ 1 << apart) for i in range(lax.axis_si...]
    unnamed x4 -> x10, local copies, waits for them, and re-layouts: 0.85 us -> 4.87 us
  transfers between devices with their start and end apart: 6 -> 0, of which waited for: 5 -> 0; matrix products, arithmetic and copies ran while one was open for 2% -> 0% of each run, Pallas kernels for 0% -> 0%
where the time goes in v1:
time: 82.2 us; the launch traced here: 81.6 us
  Pallas kernels  76.1 us (93%)
  local copies, waits for them, and re-layouts  4.87 us (6%)
    pallas_call x1, Pallas kernels, shards(): pl.pallas_call(kernel, out_shape=(jax.ShapeDtypeStruct((128, 256), BF16),...  76.1 us
    unnamed x10, local copies, waits for them, and re-layouts  4.87 us

profile of v1, /device:TPU:1, one launch (start us, length us, event | category | flops | bytes accessed | tf_op | source)
XLA Modules:
  0.0 81.6 jit_solution(12671950150642093753)
XLA Ops:
  0.6 0.0 copy-start
  0.6 0.9 %copy-done = bf16[128,768]{1,0:T(8,128)(2,1)S(1)} copy-done((bf16[128,768]{1,0:T(8,128)(2,1)S(1)}, bf16[128,768]{1,0:T(8,128)(2,1)}, u32[]{:S(2)}) %copy-start) | copy-done | bytes 196632
  1.6 0.0 copy-start.1
  1.6 0.9 %copy-done.1 = bf16[384,256]{1,0:T(8,128)(2,1)S(1)} copy-done((bf16[384,256]{1,0:T(8,128)(2,1)S(1)}, bf16[384,256]{1,0:T(8,128)(2,1)}, u32[]{:S(2)}) %copy-start.1) | copy-done | bytes 196632
  2.5 0.0 copy-start.2
  2.5 0.9 %copy-done.2 = bf16[128,768]{1,0:T(8,128)(2,1)S(1)} copy-done((bf16[128,768]{1,0:T(8,128)(2,1)S(1)}, bf16[128,768]{1,0:T(8,128)(2,1)}, u32[]{:S(2)}) %copy-start.2) | copy-done | bytes 196632
  3.4 0.0 copy-start.3
  3.4 0.8 %copy-done.3 = bf16[128,256]{1,0:T(8,128)(2,1)S(1)} copy-done((bf16[128,256]{1,0:T(8,128)(2,1)S(1)}, bf16[128,256]{1,0:T(8,128)(2,1)}, u32[]{:S(2)}) %copy-start.3) | copy-done | bytes 65560
  4.3 76.1 %layer.1 = (bf16[128,256]{1,0:T(8,128)(2,1)S(1)}, bf16[128,256]{1,0:T(8,128)(2,1)S(1)}) custom-call(bf16[128,768]{1,0:T(8,128)(2,1)S(1)} %copy-done, bf16[384,256]{1,0:T(8,128)(2,1)S(1)} %copy-done.1, bf16[128,256]{1,0:T(8,128)(2,1)S(1)} %copy-done.3, bf16[128,768]{1,0:T(8,128)(2,1)S(1)} %copy-done.2), custom_call_target="tpu_custom_call" | custom-call | flops 1700000000 | bytes 1000000 | tf_op jit(solution)/shard_map/layer/pallas_call | solution.py:301
  80.3 0.6 copy.8
  81.0 0.6 copy.9
Async XLA Ops:
  0.6 0.9 %copy-start = (bf16[128,768]{1,0:T(8,128)(2,1)S(1)}, bf16[128,768]{1,0:T(8,128)(2,1)}, u32[]{:S(2)}) copy-start(bf16[128,768]{1,0:T(8,128)(2,1)} %hid.1) | copy-start | bytes 589828
  1.6 0.9 %copy-start.1 = (bf16[384,256]{1,0:T(8,128)(2,1)S(1)}, bf16[384,256]{1,0:T(8,128)(2,1)}, u32[]{:S(2)}) copy-start(bf16[384,256]{1,0:T(8,128)(2,1)} %wd.1) | copy-start | bytes 589828
  2.5 0.9 %copy-start.2 = (bf16[128,768]{1,0:T(8,128)(2,1)S(1)}, bf16[128,768]{1,0:T(8,128)(2,1)}, u32[]{:S(2)}) copy-start(bf16[128,768]{1,0:T(8,128)(2,1)} %wq.1) | copy-start | bytes 589828
  3.4 0.8 %copy-start.3 = (bf16[128,256]{1,0:T(8,128)(2,1)S(1)}, bf16[128,256]{1,0:T(8,128)(2,1)}, u32[]{:S(2)}) copy-start(bf16[128,256]{1,0:T(8,128)(2,1)} %si.1) | copy-start | bytes 196612

commit v2 on v1

v2 whole, which is shorter than its diff:
```python
import functools

import jax
import jax.numpy as jnp
from jax import lax
from jax.experimental import pallas as pl
from jax.experimental.pallas import tpu as pltpu
from jax.sharding import PartitionSpec as P

MESH = pl.DeviceIdType.MESH
EPSILON = 1e-06
D_W = 4096
HEAD = 128
NX, NY, NZ = 4, 8, 8
F32 = jnp.float32
BF16 = jnp.bfloat16


def head_norm(parts):
    centre = parts - jnp.mean(parts, axis=-1, keepdims=True)
    spread = jnp.mean(centre * centre, axis=-1, keepdims=True)
    return centre * lax.rsqrt(spread + EPSILON)


def kernel(
    hid, wd, si, wq, out,
    wdg, ag, p1, r1, sin, sg, st, stx, sty, wqg, p2, r2, ab, acc,

    s_hid, r_hid, s_si, r_si, s_a, r_a, s_ac, r_ac, s_wd, r_wd, s_wq, r_wq, l_wd, l_wq,
    s_r1, r_r1, s_so, r_so, s_s, r_s, s_sc, r_sc, s_stx, r_stx, s_sty, r_sty, s_r2, r_r2, s_o, r_o,
):
    so, at = out.at[0], out.at[1]
    row, col = lax.axis_index("row"), lax.axis_index("col")
    z, x = lax.div(row, NX), lax.rem(row, NX)
    y, c = lax.div(col, 2), lax.rem(col, 2)
    xh, xl = lax.div(x, 2), lax.rem(x, 2)

    def dev(zz, xx, yy, cc):
        return (zz * NX + xx, yy * 2 + cc)

    up = lambda v, d, n: lax.rem(v + d + n, n)
    sibling = dev(z, x, y, 1 - c)
    yn = (dev(z, x, up(y, 1, NY), c), dev(z, x, up(y, -1, NY), c))
    zn = (dev(up(z, 1, NZ), x, y, c), dev(up(z, -1, NZ), x, y, c))
    xgroup = [dev(z, up(x, d, NX), y, e) for d in range(NX) for e in (c, 1 - c)][1:]
    ygroup = [dev(z, x, up(y, d, NY), c) for d in range(1, NY)]

    ends = []

    def remote(src, dst, ssem, rsem, to):
        copy = pltpu.make_async_remote_copy(
            src_ref=src, dst_ref=dst, send_sem=ssem, recv_sem=rsem, device_id=to, device_id_type=MESH
        )
        copy.start()
        ends.append((None, copy))
        return copy

    def sent(copy):
        ends.remove((None, copy))
        copy.wait_send()

    def within(src, dst, ssem, rsem, tx, tc):
        away = (tx != x) | (tc != c)
        copy = pltpu.make_async_remote_copy(
            src_ref=src, dst_ref=dst, send_sem=ssem, recv_sem=rsem,
            device_id=dev(z, tx, y, tc), device_id_type=MESH,
        )

        @pl.when(away)
        def _():
            copy.start()

        @pl.when(jnp.logical_not(away))
        def _():
            pltpu.make_async_copy(src, dst, rsem).start()

        ends.append((away, copy))

    def arrived(dst, rsem):
        pltpu.make_async_remote_copy(
            src_ref=dst, dst_ref=dst, send_sem=rsem, recv_sem=rsem, device_id=sibling, device_id_type=MESH
        ).wait_recv()

    tok = lambda xt: pl.ds(pl.multiple_of(xt * 128, 128), 128)

    barrier = pltpu.get_barrier_semaphore()
    greet = xgroup + ygroup + list(zn)
    for d in greet:
        pl.semaphore_signal(barrier, inc=1, device_id=d, device_id_type=MESH)
    own = [pltpu.make_async_copy(wd, wdg.at[pl.ds(pl.multiple_of(z * 384, 128), 384)], l_wd.at[0])]
    for h in range(2):
        own.append(
            pltpu.make_async_copy(
                wq.at[:, pl.ds(h * 384, 384)], wqg.at[h, pl.ds(pl.multiple_of(z * 128, 128), 128)], l_wq.at[h]
            )
        )
    for copy in own:
        copy.start()
    own[0].wait()
    pl.semaphore_wait(barrier, len(greet))

    image = (xh, 1 - xh)

    def wd_piece(j, p):
        return wdg.at[pl.ds(pl.multiple_of(j * 384 + p * 192, 64), 192)]

    def wq_piece(j, p):
        return wqg.at[p, pl.ds(pl.multiple_of(j * 128, 128), 128)]

    def a_block(j, p, k=c):
        return ag.at[j, tok(2 * image[p] + k)]

    def a_piece(j, p):
        start = pl.multiple_of((2 * image[p // 2] + c) * 128 + p % 2 * 64, 64)
        return ag.at[j, pl.ds(start, 64)]

    def s_piece(j, p, k=c):
        return sg.at[j, tok(2 * image[p] + k)]

    def block(me, s, d, n):
        return up(me, -s if d == 0 else s, n)

    def hop_send(piece, me, n, ssem, rsem, to, s, d, p, parts=2):
        j, k = block(me, s - 1, d, n), ((s - 1) * 2 + d) * parts + p
        return remote(piece(j, p), piece(j, p), ssem.at[k], rsem.at[k], to[d])

    def hop(piece, me, n, ssem, rsem, to, s, p, parts=2):
        way = p * 2 // parts
        for d in (0, 1) if s < 4 else (way,):
            arrived(piece(block(me, s, d, n), p), rsem.at[((s - 1) * 2 + d) * parts + p])
            if s < 3 or (s == 3 and d == way):
                hop_send(piece, me, n, ssem, rsem, to, s + 1, d, p, parts)

    def share(piece, ssem, rsem, s, p):
        for d in ((0, 1) if 0 < s < 4 else (p,)):
            j, k = block(y, s, d, NY), s * 4 + d * 2 + p
            remote(piece(j, p), piece(j, p), ssem.at[k], rsem.at[k], sibling)

    def shared(piece, rsem, s, p):
        for d in ((0, 1) if 0 < s < 4 else (p,)):
            arrived(piece(block(y, s, d, NY), p, 1 - c), rsem.at[s * 4 + d * 2 + p])

    def wd_hop(s, p):
        hop(wd_piece, z, NZ, s_wd, r_wd, zn, s, p)

    def wq_hop(s):
        for p in range(2):
            hop(wq_piece, z, NZ, s_wq, r_wq, zn, s, p)

    def a_hop(s, p):
        for q in range(2):
            hop(a_piece, y, NY, s_a, r_a, yn, s, 2 * p + q, 4)
        share(a_block, s_ac, r_ac, s, p)

    for h in range(2):
        for q in range(2):
            within(
                hid.at[pl.ds(64 * q, 64), pl.ds(h * 384, 384)],
                ag.at[y, pl.ds(pl.multiple_of(x * 128 + 64 * q, 64), 64)],
                s_hid.at[2 * h + q], r_hid.at[2 * xh + q], 2 * c + h, xl,
            )
    first = [hop_send(wd_piece, z, NZ, s_wd, r_wd, zn, 1, d, 0) for d in range(2)]

    def a_start(p):
        for q in range(2):
            arrived(a_piece(y, 2 * p + q), r_hid.at[2 * image[p] + q])
            for d in range(2):
                hop_send(a_piece, y, NY, s_a, r_a, yn, 1, d, 2 * p + q, 4)
        share(a_block, s_ac, r_ac, 0, p)

    a_start(0)
    for d in range(2):
        sent(first[d])
        hop_send(wd_piece, z, NZ, s_wd, r_wd, zn, 1, d, 1)
    own[1].wait()
    own[2].wait()
    for s in range(1, 4):
        wd_hop(s, 0)
        if s == 3:
            hop_send(wq_piece, z, NZ, s_wq, r_wq, zn, 1, 1, 0)
        if s == 1:
            a_start(1)
            for h in range(2):
                within(
                    si.at[:, pl.ds(h * 128, 128)], sin.at[xh], s_si.at[h], r_si.at[xh], 2 * c + h, xl
                )
        else:
            a_hop(s - 1, 1)
        wd_hop(s, 1)
        if s == 3:
            hop_send(wq_piece, z, NZ, s_wq, r_wq, zn, 1, 0, 0)
        a_hop(s, 0)
    a_hop(3, 1)
    for s in range(4):
        for p in range(2):
            shared(a_block, r_ac, s, p)

    last_a = up(y, 4, NY)
    last_w = up(z, 4, NZ)
    last_w = jnp.where(last_w == last_a, up(last_a, 1, NY), last_w)
    gap = up(last_w - last_a, NY, NY)

    def early(k):
        return up(last_a, k + (gap <= k).astype(jnp.int32), NY)

    def product(i, js):
        a = jnp.concatenate([ag[j, pl.ds(256 * i, 256), :] for j in js], axis=1)
        w = jnp.concatenate([wdg[pl.ds(pl.multiple_of(j * 384, 128), 384), :] for j in js], axis=0)
        return jnp.dot(a, w, preferred_element_type=F32)

    for i in range(2):
        acc[pl.ds(256 * i, 256), :] = product(i, [early(k) for k in range(1, 7)])
    for p in range(2):
        wd_hop(4, p)
    for d in range(2):
        hop_send(wq_piece, z, NZ, s_wq, r_wq, zn, 1, d, 1)
    for p in range(2):
        a_hop(4, p)
    for p in range(2):
        shared(a_block, r_ac, 4, p)

    for i in range(2):
        rows = pl.ds(256 * i, 256)
        p1[rows, :] = (acc[rows, :] + product(i, [last_a, last_w])).astype(BF16)
        for h in range(2):
            for e in range(2):
                within(
                    p1.at[tok(2 * i + e), pl.ds(128 * h, 128)], r1.at[x, i],
                    s_r1.at[i * 4 + h * 2 + e], r_r1.at[x * 2 + i], 2 * c + h, e,
                )
    wq_hop(1)

    lanes = lax.broadcasted_iota(jnp.int32, (8, 128), 0)
    ones = jnp.ones((8, 128), BF16)
    by_rows = lambda v: lax.dot_general(ones, v, (((1,), (1,)), ((), ())), preferred_element_type=F32)
    tile = jnp.zeros((8, 128), F32)
    image = (0, 1)
    for i in range(2):
        arrived(sin.at[i], r_si.at[i])
        total = sin[i].astype(F32)
        for xs in range(NX):
            arrived(r1.at[xs, i], r_r1.at[xs * 2 + i])
            total += r1[xs, i].astype(F32)
        stream = total.astype(BF16)
        sg[y, tok(2 * i + c), :] = stream
        for d in range(2):
            hop_send(s_piece, y, NY, s_s, r_s, yn, 1, d, i)
        share(s_piece, s_sc, r_sc, 0, i)
        wide = stream.astype(F32)
        square = wide * wide
        high = square.astype(BF16)
        low = (square - high.astype(F32)).astype(BF16)
        sums, squares = by_rows(stream), by_rows(high) + by_rows(low)
        tile = jnp.where(lanes == i, sums, jnp.where(lanes == 2 + i, squares, tile))
    stx[c * 4 + x] = tile
    for n, d in enumerate(xgroup):
        remote(stx.at[c * 4 + x], stx.at[c * 4 + x], s_stx.at[n], r_stx.at[c * 4 + x], d)
    wq_hop(2)

    def s_hop(s, p):
        hop(s_piece, y, NY, s_s, r_s, yn, s, p)
        share(s_piece, s_sc, r_sc, s, p)

    s_hop(1, 0)
    s_hop(1, 1)
    for n in range(1, 2 * NX):
        k = lax.rem(c * 4 + x + n, 8)
        arrived(stx.at[k], r_stx.at[k])
    half = lambda k: (stx[4 * k] + stx[4 * k + 1]) + (stx[4 * k + 2] + stx[4 * k + 3])
    sty[y] = jnp.where(lanes < 4, half(0), jnp.concatenate([half(1)[4:8], half(1)[0:4]], axis=0))
    for n, d in enumerate(ygroup):
        remote(sty.at[y], sty.at[y], s_sty.at[n], r_sty.at[y], d)
    s_hop(2, 0)
    s_hop(2, 1)
    for i in range(2):
        within(s_piece(y, i), so.at[:, pl.ds(pl.multiple_of(128 * xl, 128), 128)], s_so.at[i], r_so.at[xl], 2 * i + c, xh)
    wq_hop(3)
    s_hop(3, 0)
    s_hop(3, 1)
    for n in range(1, NY):
        k = lax.rem(y + n, NY)
        arrived(sty.at[k], r_sty.at[k])
    stats = sty[0]
    for j in range(1, NY):
        stats += sty[j]
    rows = []
    for xt in range(NX):
        i, k = xt // 2, xt % 2
        mean = stats[4 * k + i : 4 * k + i + 1] / D_W
        var = stats[4 * k + 2 + i : 4 * k + 3 + i] / D_W - mean * mean
        rows += [mean, lax.rsqrt(var + EPSILON)]
    st[...] = jnp.concatenate(rows + [jnp.zeros((120, 128), F32)], axis=0).T
    wq_hop(4)

    for i in range(2):
        for s in range(4):
            shared(s_piece, r_sc, s, i)
        s_hop(4, i)
        shared(s_piece, r_sc, 4, i)
        halves = []
        for k in range(2):
            xt = 2 * i + k
            mean, rstd = st[:, 2 * xt : 2 * xt + 1], st[:, 2 * xt + 1 : 2 * xt + 2]
            halves.append(
                jnp.concatenate(
                    [((sg[j, tok(xt), :].astype(F32) - mean) * rstd).astype(BF16) for j in range(NY)], axis=1
                )
            )
        normed = jnp.concatenate(halves, axis=0)
        for h in range(2):
            p2[h, i] = jnp.dot(normed, wqg[h], preferred_element_type=F32).astype(BF16)
            within(p2.at[h, i], r2.at[x], s_r2.at[2 * i + h], r_r2.at[x], 2 * c + h, i)

    total = jnp.zeros((256, 384), F32)
    for xs in range(NX):
        arrived(r2.at[xs], r_r2.at[xs])
        total += r2[xs].astype(F32)
    queries = (head_norm(total[:, 0:128]) * (1.0 / HEAD**0.5)).astype(BF16)
    keys = head_norm(total[:, 128:256]).astype(BF16)
    values = total[:, 256:384].astype(BF16)
    scores = lax.dot_general(queries, keys, (((1,), (1,)), ((), ())), preferred_element_type=F32)
    expon = jnp.exp(scores)
    probs = (expon / jnp.sum(expon, axis=-1, keepdims=True)).astype(BF16)
    ab[...] = jnp.dot(probs, values, preferred_element_type=F32).astype(BF16)
    for t in range(2):
        within(
            ab.at[pl.ds(128 * t, 128)], at.at[:, pl.ds(pl.multiple_of(128 * xl, 128), 128)],
            s_o.at[t], r_o.at[xl], 2 * c + t, xh,
        )

    for h in range(2):
        arrived(so.at[:, pl.ds(128 * h, 128)], r_so.at[h])
        arrived(at.at[:, pl.ds(128 * h, 128)], r_o.at[h])
    for away, copy in ends:
        if away is None:
            copy.wait_send()
        else:

            @pl.when(away)
            def _(copy=copy):
                copy.wait_send()


def shards(hidden, w_down, stream_in, w_qkv):
    dma = lambda *n: pltpu.SemaphoreType.DMA(n)
    vm = lambda *n: pltpu.VMEM(n, BF16)
    fm = lambda *n: pltpu.VMEM(n, F32)
    out = pl.pallas_call(
        kernel,
        out_shape=jax.ShapeDtypeStruct((2, 128, 256), BF16),
        in_specs=[pl.BlockSpec(memory_space=pltpu.HBM)] * 4,
        out_specs=pl.BlockSpec(memory_space=pltpu.HBM),
        scratch_shapes=[
            vm(3072, 256), vm(NY, 512, 384), vm(512, 256), vm(NX, 2, 128, 128), vm(2, 128, 128), vm(NY, 512, 128),
            fm(128, 128), fm(8, 8, 128), fm(NY, 8, 128), vm(2, 1024, 384), vm(2, 2, 256, 384), vm(NX, 256, 384),
            vm(256, 128), fm(512, 256),
            dma(4), dma(4), dma(2), dma(2), dma(32), dma(32), dma(20), dma(20), dma(16), dma(16), dma(16), dma(16),
            dma(1), dma(2),
            dma(8), dma(8), dma(2), dma(2), dma(16), dma(16), dma(20), dma(20), dma(7), dma(8), dma(7), dma(8),
            dma(4), dma(4), dma(2), dma(2),
        ],
        compiler_params=pltpu.CompilerParams(
            collective_id=0, has_side_effects=True, vmem_limit_bytes=56 * 1024 * 1024
        ),
        cost_estimate=pl.CostEstimate(flops=1_700_000_000, bytes_accessed=1_000_000, transcendentals=65536),
        name="layer",
    )(hidden, w_down, stream_in, w_qkv)
    return out[0], out[1]


def solution(mesh):
    placed = (P("row", "col"),) * 4
    return jax.shard_map(
        shards, mesh=mesh, in_specs=placed, out_specs=(P("row", "col"), P("row", "col")), check_vma=False
    )
```

time: 82.2 us -> 75.1 us (0.914)
  Pallas kernels: 76.1 us -> 71.8 us
  local copies, waits for them, and re-layouts: 4.87 us -> 1.53 us
    unnamed x10 -> x0, local copies, waits for them, and re-layouts: 4.87 us -> none
    pallas_call x1, Pallas kernels: 76.1 us -> 71.8 us  [shards(): pl.pallas_call(kernel, out_shape=jax.ShapeDtypeStruct((2, 128, 256), BF16...]
    squeeze x0 -> x1, local copies, waits for them, and re-layouts: none -> 1.53 us  [shards(): return (out[0], out[1])]
where the time goes in v2:
time: 75.1 us; the launch traced here: 73.9 us
  Pallas kernels  71.8 us (96%)
  local copies, waits for them, and re-layouts  1.53 us (2%)
    pallas_call x1, Pallas kernels, shards(): pl.pallas_call(kernel, out_shape=jax.ShapeDtypeStruct((2, 128, 256), BF16...  71.8 us
    squeeze x1, local copies, waits for them, and re-layouts, shards(): return (out[0], out[1])  1.53 us

profile of v2, /device:TPU:1, one launch (start us, length us, event | category | flops | bytes accessed | tf_op | source)
XLA Modules:
  0.0 73.9 jit_solution(1909906386748748065)
XLA Ops:
  0.6 71.8 %layer.1 = bf16[2,128,256]{2,1,0:T(8,128)(2,1)} custom-call(bf16[128,768]{1,0:T(8,128)(2,1)} %hid.1, bf16[384,256]{1,0:T(8,128)(2,1)} %wd.1, bf16[128,256]{1,0:T(8,128)(2,1)} %si.1, bf16[128,768]{1,0:T(8,128)(2,1)} %wq.1), custom_call_target="tpu_custom_call" | custom-call | flops 1700000000 | bytes 1000000 | tf_op jit(solution)/shard_map/layer/pallas_call | solution.py:348
  72.4 1.5 %slice_bitcast_fusion = (bf16[128,256]{1,0:T(8,128)(2,1)}, bf16[128,256]{1,0:T(8,128)(2,1)}) fusion(bf16[2,128,256]{2,1,0:T(8,128)(2,1)} %layer.1), kind=kLoop, calls=%fused_computation | loop fusion | bytes 262144 | tf_op jit(solution)/shard_map/squeeze | solution.py:368

commit v3 on v2

v3 whole, which is shorter than its diff:
```python
import jax
import jax.numpy as jnp
from jax import lax
from jax.experimental import pallas as pl
from jax.experimental.pallas import tpu as pltpu
from jax.sharding import PartitionSpec as P

MESH = pl.DeviceIdType.MESH
EPSILON = 1e-06
D_W = 4096
HEAD = 128
NX, NY, NZ = 4, 8, 8
F32 = jnp.float32
BF16 = jnp.bfloat16


def head_norm(parts):
    centre = parts - jnp.mean(parts, axis=-1, keepdims=True)
    spread = jnp.mean(centre * centre, axis=-1, keepdims=True)
    return centre * lax.rsqrt(spread + EPSILON)


def kernel(
    hid, wd, si, wq, out,
    wdg, ag, acc, p1, r1, sin, sg, st, stx, sty, wqg, p2, r2, ab,
    s_hid, r_hid, s_si, r_si, s_a, r_a, s_wd, r_wd, s_wc, r_wc, s_wq, r_wq, s_qc, r_qc, own_sem,
    s_r1, r_r1, s_so, r_so, s_s, r_s, s_stx, r_stx, s_sty, r_sty, s_r2, r_r2, s_o, r_o,
):
    so, at = out.at[0], out.at[1]
    row, col = lax.axis_index("row"), lax.axis_index("col")
    z, x = lax.div(row, NX), lax.rem(row, NX)
    y, c = lax.div(col, 2), lax.rem(col, 2)
    xh, xl = lax.div(x, 2), lax.rem(x, 2)

    def dev(zz, xx, yy, cc):
        return (zz * NX + xx, yy * 2 + cc)

    def up(v, d, n):
        return lax.rem(v + d + n, n)

    sibling = dev(z, x, y, 1 - c)
    yn2 = (dev(z, x, up(y, 2, NY), c), dev(z, x, up(y, -2, NY), c))
    yn = (dev(z, x, up(y, 1, NY), c), dev(z, x, up(y, -1, NY), c))
    zn = (dev(up(z, 1, NZ), x, y, c), dev(up(z, -1, NZ), x, y, c))
    xgroup = [dev(z, up(x, d, NX), y, e) for d in range(NX) for e in (c, 1 - c)][1:]
    ygroup = [dev(z, x, up(y, d, NY), c) for d in range(1, NY)]
    away = (2, 1, 3)

    ends = []

    def remote(src, dst, ssem, rsem, to):
        copy = pltpu.make_async_remote_copy(
            src_ref=src, dst_ref=dst, send_sem=ssem, recv_sem=rsem, device_id=to, device_id_type=MESH
        )
        copy.start()
        ends.append((None, copy))

    def drain():
        for leaves, copy in ends:
            if leaves is None:
                copy.wait_send()
            else:

                @pl.when(leaves)
                def _(copy=copy):
                    copy.wait_send()

        ends.clear()

    def within(src, dst, ssem, rsem, tx, tc):
        leaves = (tx != x) | (tc != c)
        copy = pltpu.make_async_remote_copy(
            src_ref=src, dst_ref=dst, send_sem=ssem, recv_sem=rsem,
            device_id=dev(z, tx, y, tc), device_id_type=MESH,
        )

        @pl.when(leaves)
        def _():
            copy.start()

        @pl.when(jnp.logical_not(leaves))
        def _():
            pltpu.make_async_copy(src, dst, rsem).start()

        ends.append((leaves, copy))

    def arrived(dst, rsem):
        pltpu.make_async_remote_copy(
            src_ref=dst, dst_ref=dst, send_sem=rsem, recv_sem=rsem, device_id=sibling, device_id_type=MESH
        ).wait_recv()

    barrier = pltpu.get_barrier_semaphore()
    greet = xgroup + ygroup + list(zn)
    for d in greet:
        pl.semaphore_signal(barrier, inc=1, device_id=d, device_id_type=MESH)
    own = [pltpu.make_async_copy(wd, wdg.at[c, pl.ds(pl.multiple_of(z * 384, 128), 384)], own_sem.at[0])]
    for h in range(2):
        own.append(
            pltpu.make_async_copy(
                wq.at[:, pl.ds(h * 384, 384)],
                wqg.at[2 * c + h, pl.ds(pl.multiple_of(z * 128, 128), 128)],
                own_sem.at[1 + h],
            )
        )
    for copy in own:
        copy.start()
    own[0].wait()
    pl.semaphore_wait(barrier, len(greet))

    near = jnp.where(xh == c, xl, 1 - xl)
    half = (near, 1 - near)

    def wd_piece(j, p, k=c):
        return wdg.at[k, pl.ds(pl.multiple_of(j * 384 + p * 192, 64), 192)]

    def wq_piece(j, p, k=c):
        return wqg.at[2 * k + p, pl.ds(pl.multiple_of(j * 128, 128), 128)]

    def a_piece(j, p):
        return ag.at[j, pl.ds(pl.multiple_of(half[p // 2] * 128 + p % 2 * 64, 64), 64)]

    def s_piece(j, p):
        return sg.at[j, pl.ds(128 * p, 128)]

    def block(me, s, d):
        return up(me, -s if d == 0 else s, 8)

    def hop_send(piece, me, ssem, rsem, to, s, d, p, parts=2):
        j, k = block(me, s - 1, d), ((s - 1) * 2 + d) * parts + p
        remote(piece(j, p), piece(j, p), ssem.at[k], rsem.at[k], to[d])

    def hop(piece, me, ssem, rsem, to, s, p, parts=2):
        way = p * 2 // parts
        for d in (0, 1) if s < 4 else (way,):
            arrived(piece(block(me, s, d), p), rsem.at[((s - 1) * 2 + d) * parts + p])
            if s < 3 or (s == 3 and d == way):
                hop_send(piece, me, ssem, rsem, to, s + 1, d, p, parts)

    def share(piece, ssem, rsem, s, p):
        for d in (0, 1) if 0 < s < 4 else (p,):
            j, k = block(z, s, d), s * 4 + d * 2 + p
            remote(piece(j, p), piece(j, p), ssem.at[k], rsem.at[k], sibling)

    def shared(piece, rsem, s, p):
        for d in (0, 1) if 0 < s < 4 else (p,):
            arrived(piece(block(z, s, d), p, 1 - c), rsem.at[s * 4 + d * 2 + p])

    def wd_hop(s, p):
        hop(wd_piece, z, s_wd, r_wd, zn, s, p)
        share(wd_piece, s_wc, r_wc, s, p)

    def wq_start(d, p):
        hop_send(wq_piece, z, s_wq, r_wq, zn, 1, d, p)

    def wq_hop(s, ps=(0, 1)):
        for p in ps:
            hop(wq_piece, z, s_wq, r_wq, zn, s, p)
            share(wq_piece, s_qc, r_qc, s, p)

    def a_hop(s, p):
        for q in range(2):
            hop(a_piece, y, s_a, r_a, yn, s, 2 * p + q, 4)

    def a_start(p):
        for q in range(2):
            arrived(a_piece(y, 2 * p + q), r_hid.at[2 * half[p] + q])
            for d in range(2):
                hop_send(a_piece, y, s_a, r_a, yn, 1, d, 2 * p + q, 4)

    for h in range(2):
        for q in range(2):
            within(
                hid.at[pl.ds(64 * q, 64), pl.ds(h * 384, 384)],
                ag.at[y, pl.ds(pl.multiple_of(xl * 128 + 64 * q, 64), 64)],
                s_hid.at[2 * h + q], r_hid.at[2 * xl + q], 2 * c + h, xh,
            )
    for p in range(2):
        for d in range(2):
            hop_send(wd_piece, z, s_wd, r_wd, zn, 1, d, p)
    a_start(0)
    own[1].wait()
    own[2].wait()
    for p in range(2):
        share(wd_piece, s_wc, r_wc, 0, p)
    for s in range(1, 4):
        wd_hop(s, 0)
        if s == 1:
            a_start(1)
            for h in range(2):
                within(si.at[:, pl.ds(h * 128, 128)], sin.at[xl], s_si.at[h], r_si.at[xl], 2 * c + h, xh)
        else:
            a_hop(s - 1, 1)
        wd_hop(s, 1)
        if s > 1:
            for d in range(2):
                wq_start(d, s - 2)
        a_hop(s, 0)
    a_hop(3, 1)
    wq_hop(1, (0,))
    for s in range(4):
        for p in range(2):
            shared(wd_piece, r_wc, s, p)

    last_a, last_w = up(y, 4, 8), up(z, 4, 8)
    last_w = jnp.where(last_w == last_a, up(last_a, 1, 8), last_w)
    gap = up(last_w - last_a, 8, 8)

    def product(n, js):
        a = jnp.concatenate([ag[j] for j in js], axis=1)
        w = jnp.concatenate([wdg[n, pl.ds(pl.multiple_of(j * 384, 128), 384), :] for j in js], axis=0)
        return jnp.dot(a, w, preferred_element_type=F32)

    early = [up(last_a, k + (gap <= k).astype(jnp.int32), 8) for k in range(1, 7)]
    for n in range(2):
        acc[n] = product(n, early)
    for p in range(2):
        wd_hop(4, p)
    wq_hop(1, (1,))
    for p in range(2):
        shared(wd_piece, r_wc, 4, p)
    for p in range(2):
        a_hop(4, p)

    for n in range(2):
        p1[:, pl.ds(256 * n, 256)] = (acc[n] + product(n, [last_a, last_w])).astype(BF16)

    def features(tx):
        return pl.ds(pl.multiple_of(128 * tx, 128), 128)

    for k, d in enumerate(away):
        tx = up(x, d, NX)
        remote(p1.at[:, features(tx)], r1.at[k], s_r1.at[k], r_r1.at[k], dev(z, tx, y, c))
    for p in range(2):
        share(wq_piece, s_qc, r_qc, 0, p)
    wq_hop(2)

    lanes = lax.broadcasted_iota(jnp.int32, (8, 128), 0)
    ones = jnp.ones((8, 128), BF16)

    def by_rows(v):
        return lax.dot_general(ones, v, (((1,), (1,)), ((), ())), preferred_element_type=F32)

    for t in range(2):
        arrived(sin.at[t], r_si.at[t])
    for k in range(3):
        arrived(r1.at[k], r_r1.at[k])

    def s_send(j, s, d, p, to):
        k = (s - 1) * 4 + d * 2 + p
        remote(s_piece(j, p), s_piece(j, p), s_s.at[k], r_s.at[k], to[d])

    def s_hop(s):
        for p in range(2):
            for d in (0, 1) if s < 4 else (p,):
                j = block(y, s, d)
                arrived(s_piece(j, p), r_s.at[(s - 1) * 4 + d * 2 + p])
                if s == 2:
                    s_send(j, 3, d, p, yn)
                    if d == p:
                        s_send(j, 4, d, p, yn2)

    tile = jnp.zeros((8, 128), F32)
    for t in range(2):
        rows = pl.ds(128 * t, 128)
        total = sin[t].astype(F32) + p1[rows, features(x)].astype(F32)
        for k in range(3):
            total += r1[k, rows, :].astype(F32)
        stream = total.astype(BF16)
        sg[y, rows, :] = stream
        for d in range(2):
            s_send(y, 2, d, t, yn2)
        for d in range(2):
            s_send(y, 1, d, t, yn)
        wide = stream.astype(F32)
        square = wide * wide
        high = square.astype(BF16)
        low = (square - high.astype(F32)).astype(BF16)
        sums, squares = by_rows(stream), by_rows(high) + by_rows(low)
        tile = jnp.where(lanes == t, sums, jnp.where(lanes == 2 + t, squares, tile))
    stx[3] = tile
    for k, d in enumerate(away):
        remote(stx.at[3], stx.at[k], s_stx.at[k], r_stx.at[k], dev(z, up(x, d, NX), y, c))
    wq_hop(3)
    s_hop(2)
    for k in range(3):
        arrived(stx.at[k], r_stx.at[k])
    sty[y] = (stx[0] + stx[1]) + (stx[2] + stx[3])
    for n, d in enumerate(ygroup):
        remote(sty.at[y], sty.at[y], s_sty.at[n], r_sty.at[y], d)
    wq_hop(4)
    s_hop(1)
    for t in range(2):
        within(s_piece(y, t), so.at[:, pl.ds(pl.multiple_of(128 * xl, 128), 128)], s_so.at[t], r_so.at[xl], 2 * c + t, xh)
    s_hop(3)
    for n in range(1, NY):
        k = up(y, n, NY)
        arrived(sty.at[k], r_sty.at[k])
    stats = sty[0]
    for j in range(1, NY):
        stats += sty[j]
    means = stats[0:2] / D_W
    spreads = lax.rsqrt(stats[2:4] / D_W - means * means + EPSILON)
    st[...] = jnp.concatenate([means, spreads, jnp.zeros((124, 128), F32)], axis=0).T
    for s in range(5):
        for p in range(2):
            shared(wq_piece, r_qc, s, p)
    s_hop(4)

    halves = []
    for t in range(2):
        mean, rstd = st[:, t : t + 1], st[:, 2 + t : 3 + t]
        halves.append(
            jnp.concatenate(
                [((sg[j, pl.ds(128 * t, 128), :].astype(F32) - mean) * rstd).astype(BF16) for j in range(NY)],
                axis=1,
            )
        )
    normed = jnp.concatenate(halves, axis=0)
    for k, d in enumerate(away):
        tx = up(x, d, NX)
        p2[k] = jnp.dot(normed, wqg[tx], preferred_element_type=F32).astype(BF16)
        remote(p2.at[k], r2.at[k], s_r2.at[k], r_r2.at[k], dev(z, tx, y, c))
    total = jnp.dot(normed, wqg[x], preferred_element_type=F32)
    sent = ends[-3:]
    del ends[-3:]
    drain()
    ends.extend(sent)
    for k in range(3):
        arrived(r2.at[k], r_r2.at[k])
        total += r2[k].astype(F32)
    queries = (head_norm(total[:, 0:128]) * (1.0 / HEAD**0.5)).astype(BF16)
    keys = head_norm(total[:, 128:256]).astype(BF16)
    values = total[:, 256:384].astype(BF16)
    scores = lax.dot_general(queries, keys, (((1,), (1,)), ((), ())), preferred_element_type=F32)
    expon = jnp.exp(scores)
    probs = (expon / jnp.sum(expon, axis=-1, keepdims=True)).astype(BF16)
    ab[...] = jnp.dot(probs, values, preferred_element_type=F32).astype(BF16)
    for t in range(2):
        within(
            ab.at[pl.ds(128 * t, 128)], at.at[:, pl.ds(pl.multiple_of(128 * xl, 128), 128)],
            s_o.at[t], r_o.at[xl], 2 * c + t, xh,
        )

    for h in range(2):
        arrived(so.at[:, pl.ds(128 * h, 128)], r_so.at[h])
        arrived(at.at[:, pl.ds(128 * h, 128)], r_o.at[h])
    drain()


def shards(hidden, w_down, stream_in, w_qkv):
    vm = lambda *n: pltpu.VMEM(n, BF16)
    fm = lambda *n: pltpu.VMEM(n, F32)
    counts = (4, 4, 2, 2, 32, 32, 16, 16, 20, 20, 16, 16, 20, 20, 3, 3, 3, 2, 2, 16, 16, 3, 3, 7, 8, 3, 3, 2, 2)
    out = pl.pallas_call(
        kernel,
        out_shape=jax.ShapeDtypeStruct((2, 128, 256), BF16),
        in_specs=[pl.BlockSpec(memory_space=pltpu.HBM)] * 4,
        out_specs=pl.BlockSpec(memory_space=pltpu.HBM),
        scratch_shapes=[
            vm(2, 3072, 256), vm(8, 256, 384), fm(2, 256, 256), vm(256, 512), vm(3, 256, 128), vm(2, 128, 128),
            vm(8, 256, 128), fm(128, 128), fm(4, 8, 128), fm(8, 8, 128), vm(4, 1024, 384), vm(3, 256, 384),
            vm(3, 256, 384), vm(256, 128),
            *(pltpu.SemaphoreType.DMA((n,)) for n in counts),
        ],
        compiler_params=pltpu.CompilerParams(
            collective_id=0, has_side_effects=True, vmem_limit_bytes=56 * 1024 * 1024
        ),
        cost_estimate=pl.CostEstimate(flops=1_700_000_000, bytes_accessed=1_000_000, transcendentals=65536),
        name="layer",
    )(hidden, w_down, stream_in, w_qkv)
    return out[0], out[1]


def solution(mesh):
    placed = (P("row", "col"),) * 4
    return jax.shard_map(
        shards, mesh=mesh, in_specs=placed, out_specs=(P("row", "col"), P("row", "col")), check_vma=False
    )
```

time: 75.1 us -> 73.4 us (0.977); the launches traced: 73.9 us -> 73.2 us
  Pallas kernels: 71.8 us -> 71 us
where the time goes in v3:
time: 73.4 us; the launch traced here: 73.2 us
  Pallas kernels  71 us (97%)
  local copies, waits for them, and re-layouts  1.53 us (2%)
    pallas_call x1, Pallas kernels, shards(): pl.pallas_call(kernel, out_shape=jax.ShapeDtypeStruct((2, 128, 256), BF16...  71 us
    squeeze x1, local copies, waits for them, and re-layouts, shards(): return (out[0], out[1])  1.53 us

profile of v3, /device:TPU:1, one launch (start us, length us, event | category | flops | bytes accessed | tf_op | source)
XLA Modules:
  0.0 73.2 jit_solution(6437810217307159262)
XLA Ops:
  0.6 71.0 %layer.1 = bf16[2,128,256]{2,1,0:T(8,128)(2,1)} custom-call(bf16[128,768]{1,0:T(8,128)(2,1)} %hid.1, bf16[384,256]{1,0:T(8,128)(2,1)} %wd.1, bf16[128,256]{1,0:T(8,128)(2,1)} %si.1, bf16[128,768]{1,0:T(8,128)(2,1)} %wq.1), custom_call_target="tpu_custom_call" | custom-call | flops 1700000000 | bytes 1000000 | tf_op jit(solution)/shard_map/layer/pallas_call | solution.py:354
  71.7 1.5 %slice_bitcast_fusion = (bf16[128,256]{1,0:T(8,128)(2,1)}, bf16[128,256]{1,0:T(8,128)(2,1)}) fusion(bf16[2,128,256]{2,1,0:T(8,128)(2,1)} %layer.1), kind=kLoop, calls=%fused_computation | loop fusion | bytes 262144 | tf_op jit(solution)/shard_map/squeeze | solution.py:371

commit v4 on v3

--- a/solution.py
+++ b/solution.py
@@ -22,7 +22,7 @@
 
 def kernel(
     hid, wd, si, wq, out,
-    wdg, ag, acc, p1, r1, sin, sg, st, stx, sty, wqg, p2, r2, ab,
+    wdg, ag, acc, p1, r1, sin, sg, st, stx, sty, wqg, p2, r2, ab, keep,
     s_hid, r_hid, s_si, r_si, s_a, r_a, s_wd, r_wd, s_wc, r_wc, s_wq, r_wq, s_qc, r_qc, own_sem,
     s_r1, r_r1, s_so, r_so, s_s, r_s, s_stx, r_stx, s_sty, r_sty, s_r2, r_r2, s_o, r_o,
 ):
@@ -178,17 +178,16 @@
         for d in range(2):
             hop_send(wd_piece, z, s_wd, r_wd, zn, 1, d, p)
     a_start(0)
+    a_start(1)
     own[1].wait()
     own[2].wait()
     for p in range(2):
         share(wd_piece, s_wc, r_wc, 0, p)
+    for h in range(2):
+        within(si.at[:, pl.ds(h * 128, 128)], sin.at[xl], s_si.at[h], r_si.at[xl], 2 * c + h, xh)
     for s in range(1, 4):
         wd_hop(s, 0)
-        if s == 1:
-            a_start(1)
-            for h in range(2):
-                within(si.at[:, pl.ds(h * 128, 128)], sin.at[xl], s_si.at[h], r_si.at[xl], 2 * c + h, xh)
-        else:
+        if s > 1:
             a_hop(s - 1, 1)
         wd_hop(s, 1)
         if s > 1:
@@ -205,8 +204,8 @@
     last_w = jnp.where(last_w == last_a, up(last_a, 1, 8), last_w)
     gap = up(last_w - last_a, 8, 8)
 
-    def product(n, js):
-        a = jnp.concatenate([ag[j] for j in js], axis=1)
+    def product(n, js, rows=slice(None)):
+        a = jnp.concatenate([ag[j, rows] for j in js], axis=1)
         w = jnp.concatenate([wdg[n, pl.ds(pl.multiple_of(j * 384, 128), 384), :] for j in js], axis=0)
         return jnp.dot(a, w, preferred_element_type=F32)
 
@@ -221,15 +220,19 @@
     for p in range(2):
         a_hop(4, p)
 
-    for n in range(2):
-        p1[:, pl.ds(256 * n, 256)] = (acc[n] + product(n, [last_a, last_w])).astype(BF16)
-
     def features(tx):
         return pl.ds(pl.multiple_of(128 * tx, 128), 128)
 
-    for k, d in enumerate(away):
-        tx = up(x, d, NX)
-        remote(p1.at[:, features(tx)], r1.at[k], s_r1.at[k], r_r1.at[k], dev(z, tx, y, c))
+    halves = (pl.ds(0, 128), pl.ds(128, 128))
+    for t, rows in enumerate(halves):
+        for n in range(2):
+            late = product(n, [last_a, last_w], rows)
+            p1[rows, pl.ds(256 * n, 256)] = (acc[n, rows] + late).astype(BF16)
+        for k, d in enumerate(away):
+            tx = up(x, d, NX)
+            remote(
+                p1.at[rows, features(tx)], r1.at[k, rows], s_r1.at[3 * t + k], r_r1.at[3 * t + k], dev(z, tx, y, c)
+            )
     for p in range(2):
         share(wq_piece, s_qc, r_qc, 0, p)
     wq_hop(2)
@@ -240,28 +243,25 @@
     def by_rows(v):
         return lax.dot_general(ones, v, (((1,), (1,)), ((), ())), preferred_element_type=F32)
 
-    for t in range(2):
-        arrived(sin.at[t], r_si.at[t])
-    for k in range(3):
-        arrived(r1.at[k], r_r1.at[k])
 
     def s_send(j, s, d, p, to):
         k = (s - 1) * 4 + d * 2 + p
         remote(s_piece(j, p), s_piece(j, p), s_s.at[k], r_s.at[k], to[d])
 
-    def s_hop(s):
-        for p in range(2):
-            for d in (0, 1) if s < 4 else (p,):
-                j = block(y, s, d)
-                arrived(s_piece(j, p), r_s.at[(s - 1) * 4 + d * 2 + p])
-                if s == 2:
-                    s_send(j, 3, d, p, yn)
-                    if d == p:
-                        s_send(j, 4, d, p, yn2)
+    def s_hop(s, p):
+        for d in (0, 1) if s < 4 else (p,):
+            j = block(y, s, d)
+            arrived(s_piece(j, p), r_s.at[(s - 1) * 4 + d * 2 + p])
+            if s == 2:
+                s_send(j, 3, d, p, yn)
+                if d == p:
+                    s_send(j, 4, d, p, yn2)
 
     tile = jnp.zeros((8, 128), F32)
-    for t in range(2):
-        rows = pl.ds(128 * t, 128)
+    for t, rows in enumerate(halves):
+        arrived(sin.at[t], r_si.at[t])
+        for k in range(3):
+            arrived(r1.at[k, rows], r_r1.at[3 * t + k])
         total = sin[t].astype(F32) + p1[rows, features(x)].astype(F32)
         for k in range(3):
             total += r1[k, rows, :].astype(F32)
@@ -281,17 +281,18 @@
     for k, d in enumerate(away):
         remote(stx.at[3], stx.at[k], s_stx.at[k], r_stx.at[k], dev(z, up(x, d, NX), y, c))
     wq_hop(3)
-    s_hop(2)
+    s_hop(2, 0)
     for k in range(3):
         arrived(stx.at[k], r_stx.at[k])
     sty[y] = (stx[0] + stx[1]) + (stx[2] + stx[3])
     for n, d in enumerate(ygroup):
         remote(sty.at[y], sty.at[y], s_sty.at[n], r_sty.at[y], d)
-    wq_hop(4)
-    s_hop(1)
+    s_hop(2, 1)
     for t in range(2):
         within(s_piece(y, t), so.at[:, pl.ds(pl.multiple_of(128 * xl, 128), 128)], s_so.at[t], r_so.at[xl], 2 * c + t, xh)
-    s_hop(3)
+    wq_hop(4)
+    for s in (1, 3, 4):
+        s_hop(s, 0)
     for n in range(1, NY):
         k = up(y, n, NY)
         arrived(sty.at[k], r_sty.at[k])
@@ -304,38 +305,37 @@
     for s in range(5):
         for p in range(2):
             shared(wq_piece, r_qc, s, p)
-    s_hop(4)
-
-    halves = []
-    for t in range(2):
+
+    for t, rows in enumerate(halves):
+        if t == 1:
+            for s in (1, 3, 4):
+                s_hop(s, 1)
         mean, rstd = st[:, t : t + 1], st[:, 2 + t : 3 + t]
-        halves.append(
-            jnp.concatenate(
-                [((sg[j, pl.ds(128 * t, 128), :].astype(F32) - mean) * rstd).astype(BF16) for j in range(NY)],
-                axis=1,
-            )
-        )
-    normed = jnp.concatenate(halves, axis=0)
-    for k, d in enumerate(away):
-        tx = up(x, d, NX)
-        p2[k] = jnp.dot(normed, wqg[tx], preferred_element_type=F32).astype(BF16)
-        remote(p2.at[k], r2.at[k], s_r2.at[k], r_r2.at[k], dev(z, tx, y, c))
-    total = jnp.dot(normed, wqg[x], preferred_element_type=F32)
-    sent = ends[-3:]
-    del ends[-3:]
+        normed = jnp.concatenate(
+            [((sg[j, rows, :].astype(F32) - mean) * rstd).astype(BF16) for j in range(NY)], axis=1
+        )
+        for k, d in enumerate(away):
+            tx = up(x, d, NX)
+            p2[k, rows, :] = jnp.dot(normed, wqg[tx], preferred_element_type=F32).astype(BF16)
+            remote(p2.at[k, rows], r2.at[k, rows], s_r2.at[3 * t + k], r_r2.at[3 * t + k], dev(z, tx, y, c))
+        keep[rows, :] = jnp.dot(normed, wqg[x], preferred_element_type=F32)
+    sent = ends[-6:]
+    del ends[-6:]
     drain()
     ends.extend(sent)
-    for k in range(3):
-        arrived(r2.at[k], r_r2.at[k])
-        total += r2[k].astype(F32)
-    queries = (head_norm(total[:, 0:128]) * (1.0 / HEAD**0.5)).astype(BF16)
+    for t, rows in enumerate(halves):
+        for k in range(3):
+            arrived(r2.at[k, rows], r_r2.at[3 * t + k])
+        keep[rows, :] += (r2[0, rows].astype(F32) + r2[1, rows].astype(F32)) + r2[2, rows].astype(F32)
+    total = keep[...]
     keys = head_norm(total[:, 128:256]).astype(BF16)
     values = total[:, 256:384].astype(BF16)
-    scores = lax.dot_general(queries, keys, (((1,), (1,)), ((), ())), preferred_element_type=F32)
-    expon = jnp.exp(scores)
-    probs = (expon / jnp.sum(expon, axis=-1, keepdims=True)).astype(BF16)
-    ab[...] = jnp.dot(probs, values, preferred_element_type=F32).astype(BF16)
     for t in range(2):
+        queries = (head_norm(total[128 * t : 128 * t + 128, 0:128]) * (1.0 / HEAD**0.5)).astype(BF16)
+        scores = lax.dot_general(queries, keys, (((1,), (1,)), ((), ())), preferred_element_type=F32)
+        expon = jnp.exp(scores)
+        probs = (expon / jnp.sum(expon, axis=-1, keepdims=True)).astype(BF16)
+        ab[pl.ds(128 * t, 128), :] = jnp.dot(probs, values, preferred_element_type=F32).astype(BF16)
         within(
             ab.at[pl.ds(128 * t, 128)], at.at[:, pl.ds(pl.multiple_of(128 * xl, 128), 128)],
             s_o.at[t], r_o.at[xl], 2 * c + t, xh,
@@ -350,7 +350,7 @@
 def shards(hidden, w_down, stream_in, w_qkv):
     vm = lambda *n: pltpu.VMEM(n, BF16)
     fm = lambda *n: pltpu.VMEM(n, F32)
-    counts = (4, 4, 2, 2, 32, 32, 16, 16, 20, 20, 16, 16, 20, 20, 3, 3, 3, 2, 2, 16, 16, 3, 3, 7, 8, 3, 3, 2, 2)
+    counts = (4, 4, 2, 2, 32, 32, 16, 16, 20, 20, 16, 16, 20, 20, 3, 6, 6, 2, 2, 16, 16, 3, 3, 7, 8, 6, 6, 2, 2)
     out = pl.pallas_call(
         kernel,
         out_shape=jax.ShapeDtypeStruct((2, 128, 256), BF16),
@@ -359,7 +359,7 @@
         scratch_shapes=[
             vm(2, 3072, 256), vm(8, 256, 384), fm(2, 256, 256), vm(256, 512), vm(3, 256, 128), vm(2, 128, 128),
             vm(8, 256, 128), fm(128, 128), fm(4, 8, 128), fm(8, 8, 128), vm(4, 1024, 384), vm(3, 256, 384),
-            vm(3, 256, 384), vm(256, 128),
+            vm(3, 256, 384), vm(256, 128), fm(256, 384),
             *(pltpu.SemaphoreType.DMA((n,)) for n in counts),
         ],
         compiler_params=pltpu.CompilerParams(

time: 73.4 us -> 71.9 us (0.980)
  Pallas kernels: 71 us -> 69.5 us
    pallas_call x1, Pallas kernels: 71 us -> 69.5 us  [shards(): pl.pallas_call(kernel, out_shape=jax.ShapeDtypeStruct((2, 128, 256), BF16...]
where the time goes in v4:
time: 71.9 us; the launch traced here: 71.7 us
  Pallas kernels  69.5 us (97%)
  local copies, waits for them, and re-layouts  1.53 us (2%)
    pallas_call x1, Pallas kernels, shards(): pl.pallas_call(kernel, out_shape=jax.ShapeDtypeStruct((2, 128, 256), BF16...  69.5 us
    squeeze x1, local copies, waits for them, and re-layouts, shards(): return (out[0], out[1])  1.53 us

profile of v4, /device:TPU:1, one launch (start us, length us, event | category | flops | bytes accessed | tf_op | source)
XLA Modules:
  0.0 71.7 jit_solution(8487282630836843073)
XLA Ops:
  0.6 69.5 %layer.1 = bf16[2,128,256]{2,1,0:T(8,128)(2,1)} custom-call(bf16[128,768]{1,0:T(8,128)(2,1)} %hid.1, bf16[384,256]{1,0:T(8,128)(2,1)} %wd.1, bf16[128,256]{1,0:T(8,128)(2,1)} %si.1, bf16[128,768]{1,0:T(8,128)(2,1)} %wq.1), custom_call_target="tpu_custom_call" | custom-call | flops 1700000000 | bytes 1000000 | tf_op jit(solution)/shard_map/layer/pallas_call | solution.py:354
  70.2 1.5 %slice_bitcast_fusion = (bf16[128,256]{1,0:T(8,128)(2,1)}, bf16[128,256]{1,0:T(8,128)(2,1)}) fusion(bf16[2,128,256]{2,1,0:T(8,128)(2,1)} %layer.1), kind=kLoop, calls=%fused_computation | loop fusion | bytes 262144 | tf_op jit(solution)/shard_map/squeeze | solution.py:371

commit v5 on v4

--- a/solution.py
+++ b/solution.py
@@ -353,9 +353,9 @@
     counts = (4, 4, 2, 2, 32, 32, 16, 16, 20, 20, 16, 16, 20, 20, 3, 6, 6, 2, 2, 16, 16, 3, 3, 7, 8, 6, 6, 2, 2)
     out = pl.pallas_call(
         kernel,
-        out_shape=jax.ShapeDtypeStruct((2, 128, 256), BF16),
+        out_shape=pltpu.VMEM((2, 128, 256), BF16),
         in_specs=[pl.BlockSpec(memory_space=pltpu.HBM)] * 4,
-        out_specs=pl.BlockSpec(memory_space=pltpu.HBM),
+        out_specs=pl.BlockSpec(memory_space=pltpu.VMEM),
         scratch_shapes=[
             vm(2, 3072, 256), vm(8, 256, 384), fm(2, 256, 256), vm(256, 512), vm(3, 256, 128), vm(2, 128, 128),
             vm(8, 256, 128), fm(128, 128), fm(4, 8, 128), fm(8, 8, 128), vm(4, 1024, 384), vm(3, 256, 384),

time: 71.9 us -> 70.9 us (0.986)
  local copies, waits for them, and re-layouts: 1.53 us -> 0.66 us
    squeeze x1, local copies, waits for them, and re-layouts: 1.53 us -> 0.66 us  [shards(): return (out[0], out[1])]
where the time goes in v5:
time: 70.9 us; the launch traced here: 70.7 us
  Pallas kernels  69.4 us (98%)
    pallas_call x1, Pallas kernels, shards(): pl.pallas_call(kernel, out_shape=pltpu.VMEM((2, 128, 256), BF16), in_spec...  69.4 us

profile of v5, /device:TPU:1, one launch (start us, length us, event | category | flops | bytes accessed | tf_op | source)
XLA Modules:
  0.0 70.7 jit_solution(617978759796271314)
XLA Ops:
  0.6 69.4 %layer.1 = bf16[2,128,256]{2,1,0:T(8,128)(2,1)S(1)} custom-call(bf16[128,768]{1,0:T(8,128)(2,1)} %hid.1, bf16[384,256]{1,0:T(8,128)(2,1)} %wd.1, bf16[128,256]{1,0:T(8,128)(2,1)} %si.1, bf16[128,768]{1,0:T(8,128)(2,1)} %wq.1), custom_call_target="tpu_custom_call" | custom-call | flops 1700000000 | bytes 1000000 | tf_op jit(solution)/shard_map/layer/pallas_call | solution.py:354
  70.0 0.7 slice_bitcast_fusion

commit v6 on v5

--- a/solution.py
+++ b/solution.py
@@ -167,6 +167,9 @@
             for d in range(2):
                 hop_send(a_piece, y, s_a, r_a, yn, 1, d, 2 * p + q, 4)
 
+    for p in range(2):
+        for d in range(2):
+            hop_send(wd_piece, z, s_wd, r_wd, zn, 1, d, p)
     for h in range(2):
         for q in range(2):
             within(
@@ -174,11 +177,7 @@
                 ag.at[y, pl.ds(pl.multiple_of(xl * 128 + 64 * q, 64), 64)],
                 s_hid.at[2 * h + q], r_hid.at[2 * xl + q], 2 * c + h, xh,
             )
-    for p in range(2):
-        for d in range(2):
-            hop_send(wd_piece, z, s_wd, r_wd, zn, 1, d, p)
     a_start(0)
-    a_start(1)
     own[1].wait()
     own[2].wait()
     for p in range(2):
@@ -189,6 +188,8 @@
         wd_hop(s, 0)
         if s > 1:
             a_hop(s - 1, 1)
+        else:
+            a_start(1)
         wd_hop(s, 1)
         if s > 1:
             for d in range(2):
@@ -323,21 +324,22 @@
     del ends[-6:]
     drain()
     ends.extend(sent)
+    queries, keys, values = [], [], []
     for t, rows in enumerate(halves):
         for k in range(3):
             arrived(r2.at[k, rows], r_r2.at[3 * t + k])
-        keep[rows, :] += (r2[0, rows].astype(F32) + r2[1, rows].astype(F32)) + r2[2, rows].astype(F32)
-    total = keep[...]
-    keys = head_norm(total[:, 128:256]).astype(BF16)
-    values = total[:, 256:384].astype(BF16)
-    for t in range(2):
-        queries = (head_norm(total[128 * t : 128 * t + 128, 0:128]) * (1.0 / HEAD**0.5)).astype(BF16)
-        scores = lax.dot_general(queries, keys, (((1,), (1,)), ((), ())), preferred_element_type=F32)
+        total = keep[rows, :] + (r2[0, rows].astype(F32) + r2[1, rows].astype(F32)) + r2[2, rows].astype(F32)
+        queries.append((head_norm(total[:, 0:128]) * (1.0 / HEAD**0.5)).astype(BF16))
+        keys.append(head_norm(total[:, 128:256]).astype(BF16))
+        values.append(total[:, 256:384].astype(BF16))
+    keys, values = jnp.concatenate(keys, axis=0), jnp.concatenate(values, axis=0)
+    for t, rows in enumerate(halves):
+        scores = lax.dot_general(queries[t], keys, (((1,), (1,)), ((), ())), preferred_element_type=F32)
         expon = jnp.exp(scores)
         probs = (expon / jnp.sum(expon, axis=-1, keepdims=True)).astype(BF16)
-        ab[pl.ds(128 * t, 128), :] = jnp.dot(probs, values, preferred_element_type=F32).astype(BF16)
+        ab[rows, :] = jnp.dot(probs, values, preferred_element_type=F32).astype(BF16)
         within(
-            ab.at[pl.ds(128 * t, 128)], at.at[:, pl.ds(pl.multiple_of(128 * xl, 128), 128)],
+            ab.at[rows], at.at[:, pl.ds(pl.multiple_of(128 * xl, 128), 128)],
             s_o.at[t], r_o.at[xl], 2 * c + t, xh,
         )
 

time: 70.9 us -> 70.9 us (level)
  no operation moved by 1% of the time
where the time goes in v6:
time: 70.9 us; the launch traced here: 70.7 us
  Pallas kernels  69.4 us (98%)
    pallas_call x1, Pallas kernels, shards(): pl.pallas_call(kernel, out_shape=pltpu.VMEM((2, 128, 256), BF16), in_spec...  69.4 us

profile of v6, /device:TPU:1, one launch (start us, length us, event | category | flops | bytes accessed | tf_op | source)
XLA Modules:
  0.0 70.7 jit_solution(10178237173033364446)
XLA Ops:
  0.6 69.4 %layer.1 = bf16[2,128,256]{2,1,0:T(8,128)(2,1)S(1)} custom-call(bf16[128,768]{1,0:T(8,128)(2,1)} %hid.1, bf16[384,256]{1,0:T(8,128)(2,1)} %wd.1, bf16[128,256]{1,0:T(8,128)(2,1)} %si.1, bf16[128,768]{1,0:T(8,128)(2,1)} %wq.1), custom_call_target="tpu_custom_call" | custom-call | flops 1700000000 | bytes 1000000 | tf_op jit(solution)/shard_map/layer/pallas_call | solution.py:356
  70.0 0.7 slice_bitcast_fusion

commit v7 on v5

--- a/solution.py
+++ b/solution.py
@@ -113,6 +113,9 @@
     def wd_piece(j, p, k=c):
         return wdg.at[k, pl.ds(pl.multiple_of(j * 384 + p * 192, 64), 192)]
 
+    def wd_block(j, k=c):
+        return wdg.at[k, pl.ds(pl.multiple_of(j * 384, 128), 384)]
+
     def wq_piece(j, p, k=c):
         return wqg.at[2 * k + p, pl.ds(pl.multiple_of(j * 128, 128), 128)]
 
@@ -147,7 +150,12 @@
 
     def wd_hop(s, p):
         hop(wd_piece, z, s_wd, r_wd, zn, s, p)
-        share(wd_piece, s_wc, r_wc, s, p)
+        if s == 4:
+            share(wd_piece, s_wc, r_wc, s, p)
+        elif p == 1:
+            for d in range(2):
+                j, k = block(z, s, d), s * 4 + d * 2
+                remote(wd_block(j), wd_block(j), s_wc.at[k], r_wc.at[k], sibling)
 
     def wq_start(d, p):
         hop_send(wq_piece, z, s_wq, r_wq, zn, 1, d, p)
@@ -196,9 +204,11 @@
         a_hop(s, 0)
     a_hop(3, 1)
     wq_hop(1, (0,))
-    for s in range(4):
-        for p in range(2):
-            shared(wd_piece, r_wc, s, p)
+    for p in range(2):
+        shared(wd_piece, r_wc, 0, p)
+    for s in range(1, 4):
+        for d in range(2):
+            arrived(wd_block(block(z, s, d), 1 - c), r_wc.at[s * 4 + d * 2])
 
     last_a, last_w = up(y, 4, 8), up(z, 4, 8)
     last_w = jnp.where(last_w == last_a, up(last_a, 1, 8), last_w)

time: 70.9 us -> 70.9 us (level)
  no operation moved by 1% of the time
where the time goes in v7:
time: 70.9 us; the launch traced here: 70.7 us
  Pallas kernels  69.4 us (98%)
    pallas_call x1, Pallas kernels, shards(): pl.pallas_call(kernel, out_shape=pltpu.VMEM((2, 128, 256), BF16), in_spec...  69.4 us

profile of v7, /device:TPU:1, one launch (start us, length us, event | category | flops | bytes accessed | tf_op | source)
XLA Modules:
  0.0 70.7 jit_solution(8658520507941387834)
XLA Ops:
  0.6 69.4 %layer.1 = bf16[2,128,256]{2,1,0:T(8,128)(2,1)S(1)} custom-call(bf16[128,768]{1,0:T(8,128)(2,1)} %hid.1, bf16[384,256]{1,0:T(8,128)(2,1)} %wd.1, bf16[128,256]{1,0:T(8,128)(2,1)} %si.1, bf16[128,768]{1,0:T(8,128)(2,1)} %wq.1), custom_call_target="tpu_custom_call" | custom-call | flops 1700000000 | bytes 1000000 | tf_op jit(solution)/shard_map/layer/pallas_call | solution.py:364
  70.0 0.7 slice_bitcast_fusion
